TPU v7x, 256 devices: a whole 4x4x8 slice. The times are simulated.
256 devices in a mesh: key: 64 (over z, y, core), partner: 4 (over x).
Axes of the slice: x: 4, y: 4, z: 8, core: 2. Of those that a mesh axis runs over, the one named last changes fastest.
Arguments:
- embeddings: bfloat16 [65536, 1024], P('key'), may hold values from -1 to 1
- sources: int32 [64, 256, 1], P('key', 'partner'), may hold values from 0 to 63; in each aligned block of 64 rows (0 to 63, 64 to 127, ..., all dimensions but the last counted through in order) at most 2 rows name the same one
- blocks: int32 [64, 256], P('key', 'partner'), may hold values from 0 to 63
Outputs:
- log_density: float32 [65536], P('key')
- neighbour_mean: bfloat16 [65536, 1024], P('key')
Inputs may be any that keep to these rules, and one draw needn't show every extreme that they name: `sources`: among the 64 slots of one device (aligned blocks of slots) no key range is named more than 2 times, and some key range exactly 2 times.
All inputs are finite; a program needn't handle non-finite values.
Results may differ from a plain program's by a relative error of at most 0.0034.
Values may be sent and summed in bfloat16 or wider, within the bound.
No kernel may reach another device: no remote copies, remote signals or barrier semaphores. Data moves between devices by JAX's collectives and lax.ppermute only.
A program may use at most 64 MiB of HBM per device.

v0:
```python
import jax
import jax.numpy as jnp
from jax import lax
from jax.sharding import PartitionSpec as P

D = 1024
BR = 16
CAP = 2


TEMP = 0.05


def slot_rank(source_list):
    count = source_list.shape[0]
    same = source_list[:, None] == source_list[None, :]
    before = jnp.arange(count)[None, :] < jnp.arange(count)[:, None]
    return jnp.sum(jnp.logical_and(same, before), axis=1)


def local(embeddings, sources, blocks):
    nkey = lax.axis_size("key")
    source_list = sources[0, :, 0]
    block_list = blocks[0]
    rank = slot_rank(source_list)
    keys_iota = jnp.arange(nkey, dtype=jnp.int32)
    slot_iota = jnp.arange(CAP, dtype=jnp.int32)
    place = jnp.logical_and(
        (source_list[:, None] == keys_iota)[:, :, None], (rank[:, None] == slot_iota)[:, None, :]
    )
    wanted = jnp.sum(jnp.where(place, block_list[:, None, None] + 1, 0), axis=0) - 1
    asked = lax.all_to_all(wanted, "key", split_axis=0, concat_axis=0, tiled=True)
    usable = asked >= 0
    slab_blocks = embeddings.reshape(-1, BR, D)
    outgoing = jnp.where(usable[:, :, None, None], slab_blocks[jnp.maximum(asked, 0)], 0)
    incoming = lax.all_to_all(outgoing, "key", split_axis=0, concat_axis=0, tiled=True)
    partner_rows = incoming[source_list, rank].reshape(-1, D)
    cosine = jnp.dot(embeddings, partner_rows.T, preferred_element_type=jnp.float32)
    weight = jnp.exp((cosine - 1.0) / TEMP)
    rounded = weight.astype(jnp.bfloat16)
    own_k = jnp.sum(weight, axis=1)
    own_w = jnp.dot(rounded, partner_rows, preferred_element_type=jnp.float32)
    part_k = jnp.sum(weight, axis=0).astype(jnp.bfloat16).reshape(-1, BR)
    part_w = lax.dot_general(
        rounded, embeddings, (((0,), (0,)), ((), ())), preferred_element_type=jnp.float32
    )
    part_w = part_w.astype(jnp.bfloat16).reshape(-1, BR, D)
    back_w = jnp.zeros((nkey, CAP, BR, D), jnp.bfloat16).at[source_list, rank].set(part_w)
    back_k = jnp.zeros((nkey, CAP, BR), jnp.bfloat16).at[source_list, rank].set(part_k)
    return_w, return_k = (
        lax.all_to_all(back_w, "key", split_axis=0, concat_axis=0, tiled=True),
        lax.all_to_all(back_k, "key", split_axis=0, concat_axis=0, tiled=True),
    )
    nblock = embeddings.shape[0] // BR
    target = (
        (asked[:, :, None] == jnp.arange(nblock, dtype=jnp.int32))
        .astype(jnp.bfloat16)
        .reshape(nkey * CAP, nblock)
    )
    dims = (((0,), (0,)), ((), ()))
    got_w = lax.dot_general(
        target, return_w.reshape(nkey * CAP, BR * D), dims, preferred_element_type=jnp.float32
    ).reshape(-1, D)
    got_k = lax.dot_general(
        target, return_k.reshape(nkey * CAP, BR), dims, preferred_element_type=jnp.float32
    ).reshape(-1)
    acc_w = own_w + got_w
    acc_k = own_k + got_k
    total_w, total_k = lax.psum((acc_w, acc_k), "partner")
    scale = 1.0 + total_k
    neighbour_mean = ((embeddings.astype(jnp.float32) + total_w) / scale[:, None]).astype(
        jnp.bfloat16
    )
    log_density = jnp.log(scale)
    return (log_density, neighbour_mean)


def solution(mesh):
    in_specs = (P("key", None), P("key", "partner", None), P("key", "partner"))
    out_specs = (P("key"), P("key", None))
    return jax.shard_map(local, mesh=mesh, in_specs=in_specs, out_specs=out_specs, check_vma=False)
```

profile of v0, /device:TPU:1, one launch (start us, length us, event | category | flops | bytes accessed | tf_op | source)
XLA Modules:
  0.0 398.7 jit_solution(16927126013139688699)
XLA Ops:
  7.2 0.9 convert_reduce_fusion
  8.1 0.7 iota_compare_fusion.4
  9.7 22.3 %all_to_all.24 = s32[64,1,2]{2,1,0:T(1,128)S(1)} all-to-all(s32[64,1,2]{2,1,0:T(1,128)S(1)} %copy.18), channel_id=1, replica_groups=mesh['key'=64,'partner'=4] {'key'}, dimensions={0} | all-to-all | bytes 1024 | tf_op jit(solution)/shard_map/all_to_all | solution.py:32
  32.8 0.8 fusion.19
  33.7 4.4 %gather_fusion = bf16[128,16,1024]{2,1,0:T(8,128)(2,1)} fusion(bf16[64,16,1024]{2,1,0:T(8,128)(2,1)} %bitcast.40, s32[1024]{0:T(1024)S(1)} %pad_clamp_fusion), kind=kCustom, calls=%fused_computation | custom fusion | bytes 8389120 | tf_op jit(solution)/shard_map/gather | solution.py:35
  38.1 4.5 %broadcast_select_fusion = bf16[64,2,16,1024]{3,2,1,0:T(8,128)(2,1)} fusion(bf16[64,2,16,1024]{3,2,1,0:T(8,128)(2,1)} %bitcast.41, pred[64,2]{1,0:T(8,128)(4,1)S(1)} %copy.20), kind=kLoop, calls=%fused_computation.6 | loop fusion | flops 2097152 | bytes 8388736 | tf_op jit(solution)/shard_map/jit(_where)/select_n | solution.py:35
  42.6 5.8 %all-to-all-start.1 = ((bf16[64,2,16,1024]{3,2,1,0:T(8,128)(2,1)}), bf16[64,2,16,1024]{3,2,1,0:T(8,128)(2,1)}, u32[]{:S(2)}, u32[]{:S(2)}) async-start(bf16[64,2,16,1024]{3,2,1,0:T(8,128)(2,1)} %broadcast_select_fusion), calls=%async_computation.1 | async-start | bytes 8388608 | tf_op jit(solution)/shard_map/all_to_all | solution.py:36
  48.5 94.6 %all-to-all-done.1 = bf16[64,2,16,1024]{3,2,1,0:T(8,128)(2,1)} async-done(((bf16[64,2,16,1024]{3,2,1,0:T(8,128)(2,1)}), bf16[64,2,16,1024]{3,2,1,0:T(8,128)(2,1)}, u32[]{:S(2)}, u32[]{:S(2)}) %all-to-all-start.1) | async-done | bytes 4194336 | tf_op jit(solution)/shard_map/all_to_all | solution.py:36
  143.1 4.2 %gather_fusion.1 = bf16[64,16,1024]{2,1,0:T(8,128)(2,1)} fusion(bf16[64,2,16,1024]{3,2,1,0:T(8,128)(2,1)} %all-to-all-done.1, s32[64]{0:T(128)S(1)} %bitcast.43), kind=kCustom, calls=%fused_computation.1 | custom fusion | bytes 4194816 | tf_op jit(solution)/shard_map/gather | solution.py:37
  147.3 4.4 %fusion.1 = (bf16[1024]{0:T(1024)(128)(2,1)S(1)}, f32[1024]{0:T(1024)S(1)}, f32[1024,1024]{1,0:T(8,128)S(1)}) fusion(bf16[1024,1024]{1,0:T(8,128)(2,1)} %bitcast.45, bf16[1024,1024]{1,0:T(8,128)(2,1)S(1)} %copy-done), kind=kOutput, calls=%fused_computation.8 | convolution fusion | flops 2151675904 | bytes 8394752 | tf_op jit(solution)/shard_map/dot_general | solution.py:38
  151.7 3.8 convolution_convert_fusion
  155.4 2.5 broadcast_in_dim.29
  157.9 10.7 %scatter_fusion.1 = bf16[64,2,16,1024]{3,2,1,0:T(8,128)(2,1)} fusion(bf16[64,2,16,1024]{3,2,1,0:T(8,128)(2,1)} %broadcast_in_dim.29, s32[64]{0:T(128)S(1)} %get-tuple-element.6, bf16[64,16,1024]{2,1,0:T(8,128)(2,1)} %bitcast.44), kind=kCustom, calls=%fused_computation.3 | custom fusion | bytes 6291968 | tf_op jit(solution)/shard_map/scatter | solution.py:48
  168.6 7.2 %all-to-all-start.3 = ((bf16[64,2,16,1024]{3,2,1,0:T(8,128)(2,1)}), bf16[64,2,16,1024]{3,2,1,0:T(8,128)(2,1)}, u32[]{:S(2)}, u32[]{:S(2)}) async-start(bf16[64,2,16,1024]{3,2,1,0:T(8,128)(2,1)} %scatter_fusion.1), calls=%async_computation.3 | async-start | bytes 8388608 | tf_op jit(solution)/shard_map/all_to_all | solution.py:51
  176.2 94.3 %all-to-all-done.3 = bf16[64,2,16,1024]{3,2,1,0:T(8,128)(2,1)} async-done(((bf16[64,2,16,1024]{3,2,1,0:T(8,128)(2,1)}), bf16[64,2,16,1024]{3,2,1,0:T(8,128)(2,1)}, u32[]{:S(2)}, u32[]{:S(2)}) %all-to-all-start.3) | async-done | bytes 4194336 | tf_op jit(solution)/shard_map/all_to_all | solution.py:51
  270.5 4.9 %copy.25 = bf16[16,8,16,1024]{3,1,2,0:T(8,128)(2,1)S(1)} copy(bf16[16,8,16,1024]{3,2,1,0:T(8,128)(2,1)} %bitcast.14) | data formatting | bytes 8388608
  275.4 2.8 fusion.6
  278.2 4.9 %reshape.157 = f32[1024,1024]{1,0:T(8,128)} reshape(f32[64,16384]{1,0:T(8,128)} %fusion.6) | data formatting | bytes 8388608 | tf_op jit(solution)/shard_map/reshape | solution.py:63
  283.2 8.4 %convolution_add_fusion = f32[1024,1024]{1,0:T(8,128)} fusion(f32[1024,1024]{1,0:T(8,128)} %reshape.157, bf16[1024,1024]{1,0:T(8,128)(2,1)} %bitcast.46, f32[1024,1024]{1,0:T(8,128)} %copy-done.2), kind=kOutput, calls=%fused_computation.10 | convolution fusion | flops 2151677952 | bytes 14680064 | tf_op jit(solution)/shard_map/dot_general | solution.py:42
  291.7 3.5 scatter_fusion
  295.3 16.2 %all_to_all.25 = bf16[64,2,16]{2,1,0:T(2,128)(2,1)S(1)} all-to-all(bf16[64,2,16]{2,1,0:T(2,128)(2,1)S(1)} %scatter_fusion), channel_id=1, replica_groups=mesh['key'=64,'partner'=4] {'key'}, dimensions={0} | all-to-all | bytes 8192 | tf_op jit(solution)/shard_map/all_to_all | solution.py:52
  311.8 9.8 %psum.14 = f32[1024]{0:T(1024)S(1)} all-reduce(f32[1024]{0:T(1024)S(1)} %add.75), channel_id=1, replica_groups=mesh['key'=64,'partner'=4] {'partner'}, use_global_device_ids=true, to_apply=%region_5.6 | all-reduce | flops 1024 | bytes 8192 | tf_op jit(solution)/shard_map/psum | solution.py:69
  322.1 65.3 %all-reduce.2.cloned.1.call-done = f32[1024,1024]{1,0:T(8,128)} async-done(((f32[1024,1024]{1,0:T(8,128)}), f32[1024,1024]{1,0:T(8,128)}) %all-reduce.2.cloned.1.call-update) | async-done | bytes 4194320 | tf_op jit(solution)/shard_map/psum | solution.py:69
  387.4 4.4 %divide_convert_fusion = bf16[1024,1024]{1,0:T(8,128)(2,1)} fusion(f32[1024,1024]{1,0:T(8,128)} %all-reduce.2.cloned.1.call-done, bf16[1024,1024]{1,0:T(8,128)(2,1)S(1)} %copy-done, f32[1024]{0:T(1024)S(1)} %get-tuple-element.8), kind=kLoop, calls=%fused_computation.4 | loop fusion | flops 4194304 | bytes 8392704 | tf_op jit(solution)/shard_map/convert_element_type | solution.py:71
  (27 shorter events, 3.2 us)
Async XLA Ops:
  42.6 5.9 %copy-start.1 = (s32[1,64,1]{1,2,0:T(1,128)S(1)}, s32[1,64,1]{1,2,0:T(1,128)}, u32[]{:S(2)}) copy-start(s32[1,64,1]{1,2,0:T(1,128)} %param.4) | copy-start | bytes 772
  42.6 100.5 %all-to-all-start.1 = ((bf16[64,2,16,1024]{3,2,1,0:T(8,128)(2,1)}), bf16[64,2,16,1024]{3,2,1,0:T(8,128)(2,1)}, u32[]{:S(2)}, u32[]{:S(2)}) async-start(bf16[64,2,16,1024]{3,2,1,0:T(8,128)(2,1)} %broadcast_select_fusion), calls=%async_computation.1 | async-start | bytes 8388608 | tf_op jit(solution)/shard_map/all_to_all | solution.py:36
  48.4 98.9 %copy-start = (bf16[1024,1024]{1,0:T(8,128)(2,1)S(1)}, bf16[1024,1024]{1,0:T(8,128)(2,1)}, u32[]{:S(2)}) copy-start(bf16[1024,1024]{1,0:T(8,128)(2,1)} %param.3) | copy-start | bytes 6291460
  151.7 3.8 copy-start.2
  168.6 101.9 %all-to-all-start.3 = ((bf16[64,2,16,1024]{3,2,1,0:T(8,128)(2,1)}), bf16[64,2,16,1024]{3,2,1,0:T(8,128)(2,1)}, u32[]{:S(2)}, u32[]{:S(2)}) async-start(bf16[64,2,16,1024]{3,2,1,0:T(8,128)(2,1)} %scatter_fusion.1), calls=%async_computation.3 | async-start | bytes 8388608 | tf_op jit(solution)/shard_map/all_to_all | solution.py:51
  175.8 211.6 %all-reduce.2.cloned.1.call-start = ((), (), s32[]{:S(2)}) async-start(), calls=%async_computation.4 | async-start | bytes 8388608 | tf_op jit(solution)/shard_map/psum | solution.py:69
Sparse Core Ops, SparseCore 0:
  291.7 95.6 all-reduce.1
where the time goes:
time: 399 us
  waiting for transfers between devices  254 us (64%)
  blocking collectives  48.3 us (12%)
  local copies, waits for them, and re-layouts  36.4 us (9%)
  matrix products  19.6 us (5%)
  between operations  14.1 us (4%)
  starting transfers between devices  13.3 us (3%)
  other arithmetic  12.7 us (3%)
    all_to_all x1, waiting for transfers between devices, local(): lax.all_to_all(outgoing, 'key', split_axis=0, concat_axis=0, tiled=True)  94.6 us
    all_to_all x1, waiting for transfers between devices, local(): lax.all_to_all(back_w, 'key', split_axis=0, concat_axis=0, tiled=True)  94.3 us
    psum x1, waiting for transfers between devices, local(): total_w, total_k = lax.psum((acc_w, acc_k), 'partner')  65.3 us
    all_to_all x1, blocking collectives, local(): lax.all_to_all(wanted, 'key', split_axis=0, concat_axis=0, tiled=True)  22.3 us
    all_to_all x1, blocking collectives, local(): lax.all_to_all(back_k, 'key', split_axis=0, concat_axis=0, tiled=True)  16.2 us
    scatter x1, local copies, waits for them, and re-layouts, local(): jnp.zeros((nkey, CAP, BR, D), jnp.bfloat16).at[source_list, rank]  10.7 us
    psum x1, blocking collectives, local(): total_w, total_k = lax.psum((acc_w, acc_k), 'partner')  9.77 us
    dot_general x1, matrix products, local(): own_w = jnp.dot(rounded, partner_rows, preferred_element_type=jnp.float32)  8.42 us
  transfers between devices with their start and end apart: 3, of which 3 were waited for; matrix products, arithmetic and copies ran while one was open for 1% of the time, Pallas kernels for 0%

commit v1 on v0

v1 whole, which is shorter than its diff:
```python
import jax
import jax.numpy as jnp
from jax import lax
from jax.experimental import pallas as pl
from jax.experimental.pallas import tpu as pltpu
from jax.sharding import Mesh, PartitionSpec as P

D = 1024
SLAB = 1024
BR = 16
NBLK = SLAB // BR
NBD = 64
KEYS = 64
NZ, NY, NC, NX = 8, 4, 2, 4
PIECES = NY * NC
RP = BR // PIECES
CX = D // NX
W = RP * CX
PLANE = NX * NY * NC
TEMP = 0.05

F32, BF16 = jnp.float32, jnp.bfloat16
NT = (((1,), (1,)), ((), ()))
TN = (((0,), (0,)), ((), ()))


def pair_kernel(emb_ref, inc_ref, own_ref, ownk_ref, cred_ref, credk_ref, acc_ref):
    emb = emb_ref[...]
    for y in range(NY):
        rows = []
        for c in range(NC):
            for r in range(RP):
                rows.append(
                    jnp.concatenate(
                        [
                            inc_ref[pl.ds((x * PIECES + NC * y + c) * NBD, NBD), pl.ds(r * CX, CX)]
                            for x in range(NX)
                        ],
                        axis=1,
                    )
                )
        part = jnp.concatenate(rows, axis=0)
        cosine = lax.dot_general(emb, part, NT, preferred_element_type=F32)
        weight = jnp.exp((cosine - 1.0) * (1.0 / TEMP))
        rounded = weight.astype(BF16)
        lanes = weight[:, :128] + weight[:, 128:]
        prod = jnp.dot(rounded, part, preferred_element_type=F32)
        if y == 0:
            ownk_ref[...] = lanes
            acc_ref[...] = prod
        else:
            ownk_ref[...] += lanes
            acc_ref[...] += prod
        credk_ref[pl.ds(y, 1), :] = jnp.sum(weight, axis=0, keepdims=True)
        cred = lax.dot_general(rounded, emb, TN, preferred_element_type=F32).astype(BF16)
        for c in range(NC):
            for r in range(RP):
                at = (c * RP + r) * NBD
                for x in range(NX):
                    cred_ref[pl.ds((x * PIECES + NC * y + c) * NBD, NBD), pl.ds(r * CX, CX)] = cred[
                        at : at + NBD, x * CX : (x + 1) * CX
                    ]
    for x in range(NX):
        own_ref[x] = acc_ref[:, x * CX : (x + 1) * CX].astype(BF16)


def pair_sums(emb, inc):
    return pl.pallas_call(
        pair_kernel,
        out_shape=(
            jax.ShapeDtypeStruct((NX, SLAB, CX), BF16),
            jax.ShapeDtypeStruct((SLAB, 128), F32),
            jax.ShapeDtypeStruct((PLANE * NBD, W), BF16),
            jax.ShapeDtypeStruct((NY, NC * RP * NBD), F32),
        ),
        in_specs=[pl.BlockSpec(memory_space=pltpu.VMEM)] * 2,
        out_specs=[pl.BlockSpec(memory_space=pltpu.VMEM)] * 4,
        scratch_shapes=[pltpu.VMEM((SLAB, D), F32)],
        compiler_params=pltpu.CompilerParams(vmem_limit_bytes=48 << 20),
        cost_estimate=pl.CostEstimate(
            flops=6 * SLAB * SLAB * D, bytes_accessed=10 << 20, transcendentals=SLAB * SLAB
        ),
    )(emb, inc)


def shift(axis, by):
    n = lax.axis_size(axis)
    return [(i, (i + by) % n) for i in range(n)]


def up(a, axis):
    return lax.ppermute(a, axis, shift(axis, 1))


def down(a, axis):
    return lax.ppermute(a, axis, shift(axis, -1))


def sum_over_x(own):
    me = lax.axis_index("x")
    half = SLAB // 2
    to = lambda k: lax.dynamic_index_in_dim(own, lax.rem(me + k, NX), 0, keepdims=False)
    far, right, left, mine = to(2), to(1), to(3), to(0)
    far_up, far_down = up(far[:half], "x"), down(far[half:], "x")
    from_left = [
        up((right[:half].astype(F32) + far_up.astype(F32)).astype(BF16), "x"),
        up(right[half:], "x"),
    ]
    from_right = [
        down(left[:half], "x"),
        down((left[half:].astype(F32) + far_down.astype(F32)).astype(BF16), "x"),
    ]
    return mine.astype(F32) + (
        jnp.concatenate(from_left).astype(F32) + jnp.concatenate(from_right).astype(F32)
    )


def gather_over_x(mine):
    me = lax.axis_index("x")
    half = SLAB // 2
    parts = [mine[:half], mine[half:]]
    ups = [up(p, "x") for p in parts]
    downs = [down(p, "x") for p in parts]
    far = [up(ups[0], "x"), down(downs[1], "x")]
    out = jnp.zeros((SLAB, D), BF16)
    place = lambda out, a, row, k: lax.dynamic_update_slice(
        out, a, (row, lax.rem(me + k, NX) * CX)
    )
    out = place(out, mine, 0, 0)
    for p in range(2):
        out = place(out, ups[p], p * half, 3)
        out = place(out, downs[p], p * half, 1)
        out = place(out, far[p], p * half, 2)
    return out


def local(embeddings, sources, blocks):
    me_x = lax.axis_index("x")
    me_key = lax.axis_index(("z", "y", "c"))
    columns = lax.dynamic_slice_in_dim(embeddings, me_x * CX, CX, axis=1)
    pieces = columns.reshape(NBLK, PIECES, W).transpose(1, 0, 2).reshape(PIECES * NBLK, W)
    held = lax.all_to_all(pieces, ("y", "c"), 0, 0, tiled=True)
    table = lax.all_gather(held, "z", tiled=True)

    wanted = sources[0, :, 0] * NBLK + blocks[0]
    plane_wanted = lax.all_to_all(
        jnp.broadcast_to(jnp.pad(wanted, (0, 128 - NBD)), (PLANE, 128)),
        ("x", "y", "c"), 0, 0, tiled=True,
    )[:, :NBD].reshape(-1)
    every = jnp.arange(KEYS * NBLK, dtype=jnp.int32)
    pick = (plane_wanted[:, None] == every[None, :]).astype(BF16)
    outgoing = jnp.dot(pick, table, preferred_element_type=F32).astype(BF16)
    incoming = lax.all_to_all(outgoing, ("x", "y", "c"), 0, 0, tiled=True)

    own, own_k, credit, credit_k = pair_sums(embeddings, incoming)

    back = lax.all_to_all(credit, ("x", "y", "c"), 0, 0, tiled=True)
    spread = (every[:, None] == plane_wanted[None, :]).astype(BF16)
    dense = jnp.dot(spread, back, preferred_element_type=F32).astype(BF16)
    got = lax.psum_scatter(dense, "z", tiled=True)

    own_w = sum_over_x(own)
    per_slot = credit_k.astype(BF16).reshape(NY, NC, RP, NBD).transpose(3, 0, 1, 2).reshape(NBD, BR)
    spread_k = (every[:, None] == wanted[None, :]).astype(BF16)
    dense_k = jnp.dot(spread_k, per_slot, preferred_element_type=F32).reshape(KEYS, SLAB)
    mine = jnp.arange(KEYS, dtype=jnp.int32)[:, None] == me_key
    dense_k = dense_k + jnp.where(mine, jnp.sum(own_k, axis=1)[None, :], 0.0)
    all_k = lax.all_to_all(dense_k, ("z", "y", "c"), 0, 0, tiled=True)
    total_k = lax.psum(jnp.sum(all_k, axis=0), "x")
    scale = 1.0 + total_k

    got = lax.all_to_all(got, ("y", "c"), 0, 0, tiled=True)
    got = got.reshape(PIECES, NBLK, W).transpose(1, 0, 2).reshape(SLAB, CX)
    total_w = own_w + got.astype(F32)
    mean = ((columns.astype(F32) + total_w) / scale[:, None]).astype(BF16)
    return jnp.log(scale), gather_over_x(mean)


def solution(mesh):
    fine = Mesh(mesh.devices.reshape(NZ, NY, NC, NX), ("z", "y", "c", "x"))
    key = ("z", "y", "c")
    in_specs = (P(key, None), P(key, "x", None), P(key, "x"))
    out_specs = (P(key), P(key, None))
    return jax.shard_map(local, mesh=fine, in_specs=in_specs, out_specs=out_specs, check_vma=False)
```

time: 399 us -> 293 us (0.73)
  waiting for transfers between devices: 254 us -> 91.7 us
  blocking collectives: 48.3 us -> 106 us
  local copies, waits for them, and re-layouts: 36.4 us -> 15.3 us
  starting transfers between devices: 13.3 us -> 24.7 us
  Pallas kernels: 0 us -> 11.2 us
  other arithmetic: 12.7 us -> 4.83 us
    all_to_all x2, waiting for transfers between devices: 189 us -> 9.22 us  [the longest x1 9.21 us: local(): all_k = lax.all_to_all(dense_k, ('z', 'y', 'c'), 0, 0, tiled=True)]
    psum x1 -> x0, waiting for transfers between devices: 65.3 us -> none  [local(): total_w, total_k = lax.psum((acc_w, acc_k), 'partner')]
    all_to_all x2 -> x4, blocking collectives: 38.5 us -> 95.6 us  [the longest x1 35.6 us: local(): incoming = lax.all_to_all(outgoing, ('x', 'y', 'c'), 0, 0, tiled=True)]
    all_gather x0 -> x1, waiting for transfers between devices: none -> 43.3 us  [local(): table = lax.all_gather(held, 'z', tiled=True)]
    reduce_scatter x0 -> x1, waiting for transfers between devices: none -> 27.9 us  [local(): got = lax.psum_scatter(dense, 'z', tiled=True)]
    scatter x2 -> x0, local copies, waits for them, and re-layouts: 14.2 us -> none  [the longest x1 10.7 us: local(): jnp.zeros((nkey, CAP, BR, D), jnp.bfloat16).at[source_list, rank]]
    ppermute x0 -> x12, starting transfers between devices: none -> 13.5 us  [the longest x6 11.9 us: down(): return lax.ppermute(a, axis, shift(axis, -1))]
    ppermute x0 -> x12, waiting for transfers between devices: none -> 11.3 us  [the longest x6 10.1 us: up(): return lax.ppermute(a, axis, shift(axis, 1))]
  transfers between devices with their start and end apart: 3 -> 16, of which waited for: 3 -> 7; matrix products, arithmetic and copies ran while one was open for 1% -> 5% of each run, Pallas kernels for 0% -> 0%
where the time goes in v1:
time: 293 us; the launch traced here: 291 us
  blocking collectives  106 us (36%)
  waiting for transfers between devices  91.7 us (31%)
  starting transfers between devices  24.7 us (8%)
  matrix products  23.4 us (8%)
  local copies, waits for them, and re-layouts  15.3 us (5%)
  between operations  14.3 us (5%)
  Pallas kernels  11.2 us (4%)
  other arithmetic  4.83 us (2%)
    all_gather x1, waiting for transfers between devices, local(): table = lax.all_gather(held, 'z', tiled=True)  43.3 us
    all_to_all x1, blocking collectives, local(): incoming = lax.all_to_all(outgoing, ('x', 'y', 'c'), 0, 0, tiled=True)  35.6 us
    all_to_all x1, blocking collectives, local(): back = lax.all_to_all(credit, ('x', 'y', 'c'), 0, 0, tiled=True)  31.9 us
    reduce_scatter x1, waiting for transfers between devices, local(): got = lax.psum_scatter(dense, 'z', tiled=True)  27.9 us
    all_to_all x1, blocking collectives, local(): held = lax.all_to_all(pieces, ('y', 'c'), 0, 0, tiled=True)  15.7 us
    all_to_all x1, blocking collectives, local(): lax.all_to_all(jnp.broadcast_to(jnp.pad(wanted, (0, 128 - NBD)), (PLANE,...  12.4 us
    ppermute x6, starting transfers between devices, down(): return lax.ppermute(a, axis, shift(axis, -1))  11.9 us
    dot_general x1, matrix products, local(): outgoing = jnp.dot(pick, table, preferred_element_type=F32).astype(BF16)  11.3 us
  transfers between devices with their start and end apart: 16, of which 7 were waited for; matrix products, arithmetic and copies ran while one was open for 5% of the time, Pallas kernels for 0%

profile of v1, /device:TPU:1, one launch (start us, length us, event | category | flops | bytes accessed | tf_op | source)
XLA Modules:
  0.0 291.0 jit_solution(5690449723445188630)
XLA Ops:
  8.7 15.7 %all_to_all.56 = bf16[8,64,512]{2,1,0:T(8,128)(2,1)} all-to-all(bf16[8,64,512]{2,1,0:T(8,128)(2,1)S(1)} %copy.11), channel_id=1, replica_groups=mesh['z'=8,'y'=4,'c'=2,'x'=4] {'y','c'}, dimensions={0} | all-to-all | bytes 1048576 | tf_op jit(solution)/shard_map/all_to_all | solution.py:142
  24.5 12.4 %all_to_all.57 = s32[32,1,128]{2,1,0:T(1,128)S(1)} all-to-all(s32[32,1,128]{2,1,0:T(1,128)S(1)} %broadcast_in_dim.33), channel_id=1, replica_groups=mesh['z'=8,'y'=4,'c'=2,'x'=4] {'x','y','c'}, dimensions={0} | all-to-all | bytes 32768 | tf_op jit(solution)/shard_map/all_to_all | solution.py:146
  37.0 43.3 %all-gather.2.cloned.1.call-done = bf16[4096,512]{1,0:T(8,128)(2,1)} async-done(((bf16[512,512]{1,0:T(8,128)(2,1)}), bf16[4096,512]{1,0:T(8,128)(2,1)}) %all-gather.2.cloned.1.call-update) | async-done | bytes 4194320 | tf_op jit(solution)/shard_map/all_gather | solution.py:143
  80.2 11.3 %fusion.5 = bf16[2048,512]{1,0:T(8,128)(2,1)S(1)} fusion(bf16[4096,512]{1,0:T(8,128)(2,1)} %all-gather.2.cloned.1.call-done, s32[2048]{0:T(1024)S(1)} %eq.58), kind=kOutput, calls=%fused_computation.7 | convolution fusion | flops 8599371776 | bytes 6299648 | tf_op jit(solution)/shard_map/dot_general | solution.py:152
  91.5 35.6 %all_to_all.58 = bf16[32,64,512]{2,1,0:T(8,128)(2,1)} all-to-all(bf16[32,64,512]{2,1,0:T(8,128)(2,1)S(1)} %bitcast.52), channel_id=1, replica_groups=mesh['z'=8,'y'=4,'c'=2,'x'=4] {'x','y','c'}, dimensions={0} | all-to-all | bytes 4194304 | tf_op jit(solution)/shard_map/all_to_all | solution.py:153
  127.1 11.2 %shard_map.50 = (bf16[4,1024,256]{2,1,0:T(8,128)(2,1)S(1)}, f32[1024,128]{1,0:T(8,128)S(1)}, bf16[2048,512]{1,0:T(8,128)(2,1)S(1)}, f32[4,256]{1,0:T(4,128)S(1)}) custom-call(bf16[1024,1024]{1,0:T(8,128)(2,1)} %emb_ref.1, bf16[2048,512]{1,0:T(8,128)(2,1)} %bitcast.50), custom_call_target="tpu_custom_call" | custom-call | flops 6442450944 | bytes 10485760 | tf_op jit(solution)/shard_map/pallas_call | solution.py:68
  138.2 31.9 %all_to_all.59 = bf16[32,64,512]{2,1,0:T(8,128)(2,1)S(1)} all-to-all(bf16[32,64,512]{2,1,0:T(8,128)(2,1)S(1)} %bitcast.49), channel_id=1, replica_groups=mesh['z'=8,'y'=4,'c'=2,'x'=4] {'x','y','c'}, dimensions={0} | all-to-all | bytes 4194304 | tf_op jit(solution)/shard_map/all_to_all | solution.py:157
  170.1 10.3 %fusion.4 = bf16[4096,512]{1,0:T(8,128)(2,1)} fusion(bf16[2048,512]{1,0:T(8,128)(2,1)S(1)} %bitcast.51, s32[2048]{0:T(1024)S(1)} %eq.58), kind=kOutput, calls=%fused_computation.6 | convolution fusion | flops 8600420352 | bytes 6299648 | tf_op jit(solution)/shard_map/dot_general | solution.py:159
  180.6 1.9 fusion.6
  182.5 3.1 %reshape.123 = f32[64,1,1024]{2,0,1:T(8,128)S(1)} reshape(f32[4096,16]{1,0:T(8,128)} %fusion.6) | data formatting | bytes 524288 | tf_op jit(solution)/shard_map/reshape | solution.py:165
  186.9 6.3 %all-to-all-start.3 = ((f32[64,1,1024]{2,1,0:T(1,128)}), f32[64,1,1024]{2,1,0:T(1,128)S(1)}, u32[]{:S(2)}, u32[]{:S(2)}) async-start(f32[64,1,1024]{2,1,0:T(1,128)} %copy.13), calls=%async_computation.3 | async-start | bytes 524288 | tf_op jit(solution)/shard_map/all_to_all | solution.py:168
  194.5 2.3 collective-permute-start.4
  196.8 2.7 collective-permute-start.3
  199.5 9.2 %all-to-all-done.3 = f32[64,1,1024]{2,1,0:T(1,128)S(1)} async-done(((f32[64,1,1024]{2,1,0:T(1,128)}), f32[64,1,1024]{2,1,0:T(1,128)S(1)}, u32[]{:S(2)}, u32[]{:S(2)}) %all-to-all-start.3) | async-done | bytes 262176 | tf_op jit(solution)/shard_map/all_to_all | solution.py:168
  208.7 27.9 %reduce-scatter.2.cloned.1.call-done = bf16[512,512]{1,0:T(8,128)(2,1)} async-done(((bf16[4096,512]{1,0:T(8,128)(2,1)}), bf16[512,512]{1,0:T(8,128)(2,1)}) %reduce-scatter.2.cloned.1.call-update) | async-done | bytes 524304 | tf_op jit(solution)/shard_map/reduce_scatter | solution.py:160
  236.6 4.9 %all-to-all-start.5 = ((bf16[8,64,512]{2,1,0:T(8,128)(2,1)}), bf16[8,64,512]{2,1,0:T(8,128)(2,1)S(1)}, u32[]{:S(2)}, u32[]{:S(2)}) async-start(bf16[8,64,512]{2,1,0:T(8,128)(2,1)} %bitcast.55), calls=%async_computation.6 | async-start | bytes 1048576 | tf_op jit(solution)/shard_map/all_to_all | solution.py:172
  241.5 1.9 fusion.13
  244.6 1.5 collective-permute-start.5
  246.3 10.1 %psum.7 = f32[1024]{0:T(1024)S(1)} all-reduce(f32[1024]{0:T(1024)S(1)} %reduce_sum.19), channel_id=1, replica_groups=mesh['z'=8,'y'=4,'c'=2,'x'=4] {'x'}, use_global_device_ids=true, to_apply=%region_2.3 | all-reduce | flops 1024 | bytes 8192 | tf_op jit(solution)/shard_map/psum | solution.py:169
  260.0 1.7 constant_dynamic-update-slice_fusion.3
  263.2 2.7 collective-permute-start.10
  265.9 4.4 %collective-permute-done.6 = bf16[512,256]{1,0:T(8,128)(2,1)S(1)} collective-permute-done((bf16[512,256]{1,0:T(8,128)(2,1)S(1)}, bf16[512,256]{1,0:T(8,128)(2,1)S(1)}, u32[]{:S(2)}, u32[]{:S(2)}) %collective-permute-start.6) | collective-permute-done | bytes 262176 | tf_op jit(solution)/shard_map/ppermute | solution.py:92
  270.3 2.7 collective-permute-start.11
  277.4 4.6 %collective-permute-done.9 = bf16[512,256]{1,0:T(8,128)(2,1)S(1)} collective-permute-done((bf16[512,256]{1,0:T(8,128)(2,1)S(1)}, bf16[512,256]{1,0:T(8,128)(2,1)S(1)}, u32[]{:S(2)}, u32[]{:S(2)}) %collective-permute-start.9) | collective-permute-done | bytes 262176 | tf_op jit(solution)/shard_map/ppermute | solution.py:92
  (58 shorter events, 17.4 us)
Async XLA Ops:
  7.2 73.0 %all-gather.2.cloned.1.call-start = ((), (), s32[]{:S(2)}) async-start(), calls=%async_computation.7 | async-start | bytes 4718592 | tf_op jit(solution)/shard_map/all_gather | solution.py:143
  8.3 16.1 %copy-start.2 = (s32[1,64]{1,0:T(1,128)S(1)}, s32[1,64]{1,0:T(1,128)}, u32[]{:S(2)}) copy-start(s32[1,64]{1,0:T(1,128)} %param.5) | copy-start | bytes 772
  8.3 16.1 %copy-start.3 = (s32[1,64,1]{1,2,0:T(1,128)S(1)}, s32[1,64,1]{1,2,0:T(1,128)}, u32[]{:S(2)}) copy-start(s32[1,64,1]{1,2,0:T(1,128)} %param.4) | copy-start | bytes 772
  24.4 212.3 %reduce-scatter.2.cloned.1.call-start = ((), (), s32[]{:S(2)}) async-start(), calls=%async_computation.8 | async-start | bytes 4718592 | tf_op jit(solution)/shard_map/reduce_scatter | solution.py:160
  186.9 21.8 %all-to-all-start.3 = ((f32[64,1,1024]{2,1,0:T(1,128)}), f32[64,1,1024]{2,1,0:T(1,128)S(1)}, u32[]{:S(2)}, u32[]{:S(2)}) async-start(f32[64,1,1024]{2,1,0:T(1,128)} %copy.13), calls=%async_computation.3 | async-start | bytes 524288 | tf_op jit(solution)/shard_map/all_to_all | solution.py:168
  194.1 47.4 %collective-permute-start = (bf16[512,256]{1,0:T(8,128)(2,1)}, bf16[512,256]{1,0:T(8,128)(2,1)S(1)}, u32[]{:S(2)}, u32[]{:S(2)}) collective-permute-start(bf16[512,256]{1,0:T(8,128)(2,1)} %get-tuple-element.14), channel_id=1, source_target_pairs={{0,1},{1,2},{2,3},{3,0},{4,5},{5,6},{6,7},{7,4},{8,9},{9,10},{10,1... | collective-permute-start | bytes 786440 | tf_op jit(solution)/shard_map/ppermute | solution.py:92
  194.5 47.1 %collective-permute-start.4 = (bf16[512,256]{1,0:T(8,128)(2,1)}, bf16[512,256]{1,0:T(8,128)(2,1)}, u32[]{:S(2)}, u32[]{:S(2)}) collective-permute-start(bf16[512,256]{1,0:T(8,128)(2,1)} %get-tuple-element.16), channel_id=1, source_target_pairs={{0,3},{1,0},{2,1},{3,2},{4,7},{5,4},{6,5},{7,6},{8,11},{9,8},{10,9... | collective-permute-start | bytes 786440 | tf_op jit(solution)/shard_map/ppermute | solution.py:96
  196.8 62.0 %collective-permute-start.2 = (bf16[512,256]{1,0:T(8,128)(2,1)}, bf16[512,256]{1,0:T(8,128)(2,1)}, u32[]{:S(2)}, u32[]{:S(2)}) collective-permute-start(bf16[512,256]{1,0:T(8,128)(2,1)} %get-tuple-element.17), channel_id=1, source_target_pairs={{0,1},{1,2},{2,3},{3,0},{4,5},{5,6},{6,7},{7,4},{8,9},{9,10},{10,1... | collective-permute-start | bytes 786440 | tf_op jit(solution)/shard_map/ppermute | solution.py:92
  196.8 62.0 %collective-permute-start.3 = (bf16[512,256]{1,0:T(8,128)(2,1)S(1)}, bf16[512,256]{1,0:T(8,128)(2,1)}, u32[]{:S(2)}, u32[]{:S(2)}) collective-permute-start(bf16[512,256]{1,0:T(8,128)(2,1)S(1)} %get-tuple-element.15), channel_id=1, source_target_pairs={{0,3},{1,0},{2,1},{3,2},{4,7},{5,4},{6,5},{7,6},{8,11},{9,8},{10,9... | collective-permute-start | bytes 786440 | tf_op jit(solution)/shard_map/ppermute | solution.py:96
  236.6 20.3 %all-to-all-start.5 = ((bf16[8,64,512]{2,1,0:T(8,128)(2,1)}), bf16[8,64,512]{2,1,0:T(8,128)(2,1)S(1)}, u32[]{:S(2)}, u32[]{:S(2)}) async-start(bf16[8,64,512]{2,1,0:T(8,128)(2,1)} %bitcast.55), calls=%async_computation.6 | async-start | bytes 1048576 | tf_op jit(solution)/shard_map/all_to_all | solution.py:172
  243.4 15.4 %collective-permute-start.1 = (bf16[512,256]{1,0:T(8,128)(2,1)}, bf16[512,256]{1,0:T(8,128)(2,1)}, u32[]{:S(2)}, u32[]{:S(2)}) collective-permute-start(bf16[512,256]{1,0:T(8,128)(2,1)} %get-tuple-element.12), channel_id=1, source_target_pairs={{0,1},{1,2},{2,3},{3,0},{4,5},{5,6},{6,7},{7,4},{8,9},{9,10},{10,1... | collective-permute-start | bytes 786440 | tf_op jit(solution)/shard_map/ppermute | solution.py:92
  244.6 14.2 %collective-permute-start.5 = (bf16[512,256]{1,0:T(8,128)(2,1)}, bf16[512,256]{1,0:T(8,128)(2,1)}, u32[]{:S(2)}, u32[]{:S(2)}) collective-permute-start(bf16[512,256]{1,0:T(8,128)(2,1)} %get-tuple-element.13), channel_id=1, source_target_pairs={{0,3},{1,0},{2,1},{3,2},{4,7},{5,4},{6,5},{7,6},{8,11},{9,8},{10,9... | collective-permute-start | bytes 786440 | tf_op jit(solution)/shard_map/ppermute | solution.py:96
  258.8 1.2 copy-start
  261.8 1.3 copy-start.1
  263.1 7.1 %collective-permute-start.6 = (bf16[512,256]{1,0:T(8,128)(2,1)S(1)}, bf16[512,256]{1,0:T(8,128)(2,1)S(1)}, u32[]{:S(2)}, u32[]{:S(2)}) collective-permute-start(bf16[512,256]{1,0:T(8,128)(2,1)S(1)} %get-tuple-element.19), channel_id=1, source_target_pairs={{0,1},{1,2},{2,3},{3,0},{4,5},{5,6},{6,7},{7,4},{8,9},{9,10},{10,1... | collective-permute-start | bytes 786440 | tf_op jit(solution)/shard_map/ppermute | solution.py:92
  263.2 7.1 %collective-permute-start.10 = (bf16[512,256]{1,0:T(8,128)(2,1)S(1)}, bf16[512,256]{1,0:T(8,128)(2,1)S(1)}, u32[]{:S(2)}, u32[]{:S(2)}) collective-permute-start(bf16[512,256]{1,0:T(8,128)(2,1)S(1)} %get-tuple-element.18), channel_id=1, source_target_pairs={{0,3},{1,0},{2,1},{3,2},{4,7},{5,4},{6,5},{7,6},{8,11},{9,8},{10,9... | collective-permute-start | bytes 786440 | tf_op jit(solution)/shard_map/ppermute | solution.py:96
  265.9 9.0 %collective-permute-start.7 = (bf16[512,256]{1,0:T(8,128)(2,1)S(1)}, bf16[512,256]{1,0:T(8,128)(2,1)S(1)}, u32[]{:S(2)}, u32[]{:S(2)}) collective-permute-start(bf16[512,256]{1,0:T(8,128)(2,1)S(1)} %get-tuple-element.19), channel_id=1, source_target_pairs={{0,3},{1,0},{2,1},{3,2},{4,7},{5,4},{6,5},{7,6},{8,11},{9,8},{10,9... | collective-permute-start | bytes 786440 | tf_op jit(solution)/shard_map/ppermute | solution.py:96
  270.3 6.4 %collective-permute-start.8 = (bf16[512,256]{1,0:T(8,128)(2,1)S(1)}, bf16[512,256]{1,0:T(8,128)(2,1)S(1)}, u32[]{:S(2)}, u32[]{:S(2)}) collective-permute-start(bf16[512,256]{1,0:T(8,128)(2,1)S(1)} %collective-permute-done.6), channel_id=1, source_target_pairs={{0,1},{1,2},{2,3},{3,0},{4,5},{5,6},{6,7},{7,4},{8,9},{9,10},{10,1... | collective-permute-start | bytes 786440 | tf_op jit(solution)/shard_map/ppermute | solution.py:92
  270.3 11.8 %collective-permute-start.9 = (bf16[512,256]{1,0:T(8,128)(2,1)S(1)}, bf16[512,256]{1,0:T(8,128)(2,1)S(1)}, u32[]{:S(2)}, u32[]{:S(2)}) collective-permute-start(bf16[512,256]{1,0:T(8,128)(2,1)S(1)} %get-tuple-element.18), channel_id=1, source_target_pairs={{0,1},{1,2},{2,3},{3,0},{4,5},{5,6},{6,7},{7,4},{8,9},{9,10},{10,1... | collective-permute-start | bytes 786440 | tf_op jit(solution)/shard_map/ppermute | solution.py:92
  270.3 13.2 %collective-permute-start.11 = (bf16[512,256]{1,0:T(8,128)(2,1)S(1)}, bf16[512,256]{1,0:T(8,128)(2,1)S(1)}, u32[]{:S(2)}, u32[]{:S(2)}) collective-permute-start(bf16[512,256]{1,0:T(8,128)(2,1)S(1)} %collective-permute-done.10), channel_id=1, source_target_pairs={{0,3},{1,0},{2,1},{3,2},{4,7},{5,4},{6,5},{7,6},{8,11},{9,8},{10,9... | collective-permute-start | bytes 786440 | tf_op jit(solution)/shard_map/ppermute | solution.py:96
Sparse Core Ops, SparseCore 0:
  24.5 55.6 all-gather.1
  180.6 55.9 reduce-scatter.1

commit v2 on v1

v2 whole, which is shorter than its diff:
```python
import functools

import jax
import jax.numpy as jnp
from jax import lax
from jax.experimental import pallas as pl
from jax.experimental.pallas import tpu as pltpu
from jax.sharding import Mesh, PartitionSpec as P

D = 1024
SLAB = 1024
BR = 16
CAP = 2
NBLK = SLAB // BR
NBD = 64
KEYS = 64
NZ, NY, NC, NX = 8, 4, 2, 4
PEERS = NY * NC
PLANE = NX * PEERS
CX = D // NX
TEMP = 0.05
GROUPS = ((0, 1, 7), (2, 6), (3, 4, 5))

F32, BF16, I32 = jnp.float32, jnp.bfloat16, jnp.int32
NT = (((1,), (1,)), ((), ()))
TN = (((0,), (0,)), ((), ()))
SMEM = pl.BlockSpec(memory_space=pltpu.SMEM)


def pick_kernel(count, asked_ref, *refs):
    tables, out_ref = refs[:count], refs[count]
    for k, table_ref in enumerate(tables):

        def body(n, _, k=k, table_ref=table_ref):
            at = (n // CAP) * (count * CAP) + k * CAP + n % CAP
            out_ref[at] = table_ref[jnp.maximum(asked_ref[k, n], 0)]
            return 0

        lax.fori_loop(0, PLANE * CAP, body, 0)


def pick_blocks(asked, tables):
    count = len(tables)
    out = pl.pallas_call(
        functools.partial(pick_kernel, count),
        out_shape=jax.ShapeDtypeStruct((PLANE * count * CAP, BR, CX), BF16),
        in_specs=[SMEM] + [pl.BlockSpec(memory_space=pltpu.VMEM)] * count,
        out_specs=pl.BlockSpec(memory_space=pltpu.VMEM),
        compiler_params=pltpu.CompilerParams(vmem_limit_bytes=12 << 20),
        cost_estimate=pl.CostEstimate(flops=0, bytes_accessed=count << 20, transcendentals=0),
    )(asked, *[t.reshape(NBLK, BR, CX) for t in tables])
    return out.reshape(-1, CX)


def pair_kernel(group_ref, place_ref, emb_ref, *refs):
    count = len(GROUPS)
    inc_refs, (part_ref, rounded_ref, ownk_ref, credk_ref) = refs[:count], refs[count : count + 4]
    cred_refs, held_ref = refs[count + 4 : 2 * count + 4], refs[2 * count + 4]
    emb = emb_ref[...]
    slots = 16
    rows = slots * BR

    for g in range(count):
        cred_refs[g][...] = jnp.zeros_like(cred_refs[g])

    for first in range(0, NBD, slots):

        def fetch(j, _, first=first):
            at = pl.ds(pl.multiple_of((first + j) * BR, BR), BR)
            for g in range(count):

                @pl.when(group_ref[first + j] == g)
                def _(g=g):
                    for x in range(NX):
                        place = x * (inc_refs[g].shape[0] // NX) + place_ref[first + j]
                        part_ref[at, pl.ds(x * CX, CX)] = inc_refs[g][place]

            return 0

        lax.fori_loop(0, slots, fetch, 0)
        part = part_ref[pl.ds(first * BR, rows), :]
        cosine = lax.dot_general(emb, part, NT, preferred_element_type=F32)
        weight = jnp.exp((cosine - 1.0) * (1.0 / TEMP))
        rounded = weight.astype(BF16)
        rounded_ref[:, pl.ds(first * BR, rows)] = rounded
        lanes = weight[:, :128] + weight[:, 128:]
        if first == 0:
            ownk_ref[...] = lanes
        else:
            ownk_ref[...] += lanes
        credk_ref[:, pl.ds(first * BR, rows)] = jnp.sum(weight, axis=0, keepdims=True)
        held_ref[...] = lax.dot_general(rounded, emb, TN, preferred_element_type=F32).astype(BF16)

        def store(j, _, first=first):
            at = pl.ds(pl.multiple_of(j * BR, BR), BR)
            for g in range(count):

                @pl.when(group_ref[first + j] == g)
                def _(g=g):
                    for x in range(NX):
                        place = x * (cred_refs[g].shape[0] // NX) + place_ref[first + j]
                        cred_refs[g][place] = held_ref[at, pl.ds(x * CX, CX)]

            return 0

        lax.fori_loop(0, slots, store, 0)


def pair_weights(group, place, emb, incoming):
    shapes = [jax.ShapeDtypeStruct((PLANE * len(ks) * CAP, BR, CX), BF16) for ks in GROUPS]
    incoming = [a.reshape(s.shape) for a, s in zip(incoming, shapes)]
    out = pl.pallas_call(
        pair_kernel,
        out_shape=(
            pltpu.HBM((SLAB, D), BF16),
            pltpu.HBM((SLAB, SLAB), BF16),
            jax.ShapeDtypeStruct((SLAB, 128), F32),
            jax.ShapeDtypeStruct((1, SLAB), F32),
            *[pltpu.HBM(s.shape, s.dtype) for s in shapes],
        ),
        in_specs=[SMEM, SMEM] + [pl.BlockSpec()] * (1 + len(GROUPS)),
        scratch_shapes=[pltpu.VMEM((16 * BR, D), BF16)],
        compiler_params=pltpu.CompilerParams(vmem_limit_bytes=28 << 20),
        cost_estimate=pl.CostEstimate(
            flops=4 * SLAB * SLAB * D, bytes_accessed=14 << 20, transcendentals=SLAB * SLAB
        ),
    )(group, place, emb, *incoming)
    return out[:4], [a.reshape(-1, CX) for a in out[4:]]


def own_kernel(rounded_ref, part_ref, own_ref):
    own_ref[0] = jnp.dot(rounded_ref[...], part_ref[...], preferred_element_type=F32).astype(BF16)


def own_sums(rounded, part):
    return pl.pallas_call(
        own_kernel,
        grid=(NX,),
        out_shape=pltpu.HBM((NX, SLAB, CX), BF16),
        in_specs=[
            pl.BlockSpec((SLAB, SLAB), lambda x: (0, 0)),
            pl.BlockSpec((SLAB, CX), lambda x: (0, x)),
        ],
        out_specs=pl.BlockSpec((1, SLAB, CX), lambda x: (x, 0, 0)),
        compiler_params=pltpu.CompilerParams(vmem_limit_bytes=12 << 20),
        cost_estimate=pl.CostEstimate(
            flops=2 * SLAB * SLAB * D, bytes_accessed=6 << 20, transcendentals=0
        ),
    )(*[pltpu.with_memory_space_constraint(a, pltpu.HBM) for a in (rounded, part)])


def add_kernel(count, ks, firsts, asked_ref, back_ref, *refs):
    n_out = len(ks)
    recvs, outs, acc_ref = refs[: len(firsts)], refs[len(firsts) : -1], refs[-1]
    for i, k in enumerate(ks):
        acc_ref[...] = jnp.zeros_like(acc_ref)
        for n, (recv, (target, first)) in enumerate(zip(recvs, firsts)):
            if target == i:
                acc_ref[pl.ds(first, recv.shape[0])] += recv[...].astype(F32)

        def body(n, _, k=k):
            block = asked_ref[k, n]

            @pl.when(block >= 0)
            def _():
                at = (n // CAP) * (count * CAP) + k * CAP + n % CAP
                acc_ref[block] += back_ref[at].astype(F32)

            return 0

        lax.fori_loop(0, PLANE * CAP, body, 0)
        if n_out == 1 and len(outs) == 2:
            outs[0][...] = acc_ref[: NBLK // 2].astype(outs[0].dtype)
            outs[1][...] = acc_ref[NBLK // 2 :].astype(outs[1].dtype)
        else:
            outs[i][...] = acc_ref[...].astype(outs[i].dtype)


def add_credits(asked, back, count, ks, recvs, firsts, outs):
    vmem = pl.BlockSpec(memory_space=pltpu.VMEM)
    return pl.pallas_call(
        functools.partial(add_kernel, count, tuple(ks), tuple(firsts)),
        out_shape=tuple(jax.ShapeDtypeStruct((n, BR, CX), t) for n, t in outs),
        in_specs=[SMEM, vmem] + [vmem] * len(recvs),
        out_specs=(vmem,) * len(outs),
        scratch_shapes=[pltpu.VMEM((NBLK, BR, CX), F32)],
        compiler_params=pltpu.CompilerParams(vmem_limit_bytes=12 << 20),
        cost_estimate=pl.CostEstimate(
            flops=0, bytes_accessed=(2 + len(ks)) << 20, transcendentals=0
        ),
    )(asked, back.reshape(-1, BR, CX), *[r.reshape(-1, BR, CX) for r in recvs])


def shift(axis, by):
    n = lax.axis_size(axis)
    return [(i, (i + by) % n) for i in range(n)]


def up(a, axis):
    return lax.ppermute(a, axis, shift(axis, 1))


def down(a, axis):
    return lax.ppermute(a, axis, shift(axis, -1))


def in_plane(a):
    return lax.all_to_all(a, ("x", "y", "c"), 0, 0, tiled=True)


def gather_over_x(mine):
    me = lax.axis_index("x")
    half = SLAB // 2
    parts = [mine[:half], mine[half:]]
    ups = [up(p, "x") for p in parts]
    downs = [down(p, "x") for p in parts]
    far = [up(ups[0], "x"), down(downs[1], "x")]
    place = lambda out, a, row, k: lax.dynamic_update_slice(
        out, a, (row, lax.rem(me + k, NX) * CX)
    )
    out = jnp.concatenate([mine] * NX, axis=1)
    for p in range(2):
        out = place(out, ups[p], p * half, 3)
        out = place(out, downs[p], p * half, 1)
        out = place(out, far[p], p * half, 2)
    return out


def slot_rank(source_list):
    count = source_list.shape[0]
    same = source_list[:, None] == source_list[None, :]
    before = jnp.arange(count)[None, :] < jnp.arange(count)[:, None]
    return jnp.sum(jnp.logical_and(same, before), axis=1).astype(I32)


def local(embeddings, sources, blocks):
    me_x, me_z = lax.axis_index("x"), lax.axis_index("z")
    columns = lax.dynamic_slice_in_dim(embeddings, me_x * CX, CX, axis=1)
    half = SLAB // 2

    source, block = sources[0, :, 0], blocks[0]
    rank = slot_rank(source)
    far = lax.rem(source // PEERS - me_z + NZ, NZ)
    peer = source % PEERS
    cell = (peer * NZ + far) * CAP + rank
    cells = jnp.arange(KEYS * CAP, dtype=I32)
    wanted = jnp.sum(jnp.where(cell[:, None] == cells[None, :], block[:, None] + 1, 0), axis=0) - 1
    wanted = jnp.tile(wanted.reshape(PEERS, NZ * CAP), (NX, 1))
    asked = in_plane(jnp.pad(wanted, ((0, 0), (0, 128 - NZ * CAP))))[:, : NZ * CAP]
    asked = asked.reshape(PLANE, NZ, CAP).transpose(1, 0, 2).reshape(NZ, PLANE * CAP)

    tables = {0: columns}
    ups = downs = columns
    for step in range(1, NZ // 2):
        ups, downs = up(ups, "z"), down(downs, "z")
        tables[NZ - step], tables[step] = ups, downs
    tables[NZ // 2] = jnp.concatenate([up(ups[:half], "z"), down(downs[half:], "z")])
    asked_of = [jnp.stack([asked[k] for k in ks]) for ks in GROUPS]
    incoming = [
        in_plane(pick_blocks(a, [tables[k] for k in ks])) for a, ks in zip(asked_of, GROUPS)
    ]

    group, place = jnp.zeros_like(far), jnp.zeros_like(far)
    for g, ks in enumerate(GROUPS):
        for n, k in enumerate(ks):
            group = jnp.where(far == k, g, group)
            place = jnp.where(far == k, (peer * len(ks) + n) * CAP + rank, place)
    (part, rounded, own_k, credit_k), credits = pair_weights(group, place, embeddings, incoming)

    back = [None] * len(GROUPS)
    last = len(GROUPS) - 1
    back[last] = in_plane(credits[last])
    own = own_sums(rounded, part)
    own_w = lax.psum_scatter(own, "x", tiled=True)[0]

    per_slot = credit_k.astype(BF16).reshape(NBD, BR)
    every = jnp.arange(KEYS * NBLK, dtype=I32)
    spread_k = ((source * NBLK + block)[:, None] == every[None, :]).astype(BF16)
    dense_k = lax.dot_general(per_slot, spread_k, TN, preferred_element_type=F32)

    assert all(k in ks and NZ - k in ks for k, ks in zip((1, 2, 3), GROUPS))
    where = {k: (g, n) for g, ks in enumerate(GROUPS) for n, k in enumerate(ks)}

    def add(ks, recvs, firsts, outs):
        g = where[ks[0]][0]
        return add_credits(
            asked_of[g], back[g], len(GROUPS[g]), [where[k][1] for k in ks], recvs, firsts, outs
        )

    to_up, to_down = add([NZ // 2], [], [], [(NBLK // 2, BF16)] * 2)
    for k in range(NZ // 2 - 1, 0, -1):
        if k > 1:
            to_up, to_down, credit = lax.optimization_barrier((to_up, to_down, credits[k - 2]))
            back[k - 2] = in_plane(credit)
        from_down, from_up = up(to_up, "z"), down(to_down, "z")
        firsts = [(0, 0), (1, NBLK // 2 if k == NZ // 2 - 1 else 0)]
        to_up, to_down = add([k, NZ - k], [from_down, from_up], firsts, [(NBLK, BF16)] * 2)
        if k == 2:
            to_up, to_down, dense_k = lax.optimization_barrier((to_up, to_down, dense_k))
    from_down, from_up = up(to_up, "z"), down(to_down, "z")
    (got,) = add([0], [from_down, from_up], [(0, 0), (0, 0)], [(NBLK, F32)])

    all_k = lax.all_to_all(dense_k.reshape(BR, KEYS, NBLK), ("z", "y", "c"), 1, 0, tiled=True)
    got_k = jnp.sum(all_k.reshape(KEYS, BR, NBLK), axis=0).T.reshape(SLAB)
    scale = 1.0 + lax.psum(got_k + jnp.sum(own_k, axis=1), "x")

    got, own_w, scale = lax.optimization_barrier((got, own_w, scale))
    total_w = own_w.astype(F32) + got.reshape(SLAB, CX)
    mean = ((columns.astype(F32) + total_w) / scale[:, None]).astype(BF16)
    return jnp.log(scale), gather_over_x(lax.optimization_barrier(mean))


def solution(mesh):
    fine = Mesh(mesh.devices.reshape(NZ, NY, NC, NX), ("z", "y", "c", "x"))
    key = ("z", "y", "c")
    in_specs = (P(key, None), P(key, "x", None), P(key, "x"))
    out_specs = (P(key), P(key, None))
    return jax.shard_map(local, mesh=fine, in_specs=in_specs, out_specs=out_specs, check_vma=False)
```

time: 293 us -> 306 us (1.044)
  blocking collectives: 106 us -> 55.2 us
  starting transfers between devices: 24.7 us -> 64.9 us
  Pallas kernels: 11.2 us -> 51.3 us
  matrix products: 23.4 us -> 0.35 us
    all_to_all x4 -> x2, blocking collectives: 95.6 us -> 46.7 us  [in_plane(): return lax.all_to_all(a, ('x', 'y', 'c'), 0, 0, tiled=True)]
    ppermute x6 -> x11, waiting for transfers between devices: 10.1 us -> 56.4 us  [up(): return lax.ppermute(a, axis, shift(axis, 1))]
    all_gather x1 -> x0, waiting for transfers between devices: 43.3 us -> none  [local(): table = lax.all_gather(held, 'z', tiled=True)]
    pallas_call x1 -> x10, Pallas kernels: 11.2 us -> 51.3 us  [the longest x1 18.5 us: pair_weights(): pl.pallas_call(pair_kernel, out_shape=(pltpu.HBM((SLAB, D), BF16), pltpu....]
    reduce_scatter x1, waiting for transfers between devices: 27.9 us -> 0.02 us  [local(): own_w = lax.psum_scatter(own, 'x', tiled=True)[0]]
    all_to_all x2 -> x6, waiting for transfers between devices: 9.22 us -> 35.2 us  [the longest x5 29.4 us: in_plane(): return lax.all_to_all(a, ('x', 'y', 'c'), 0, 0, tiled=True)]
    dot_general x3 -> x1, matrix products: 23.4 us -> 0.35 us  [local(): lax.dot_general(per_slot, spread_k, TN, preferred_element_type=F32)]
    all_to_all x2 -> x6, starting transfers between devices: 11.1 us -> 33.1 us  [the longest x5 22 us: in_plane(): return lax.all_to_all(a, ('x', 'y', 'c'), 0, 0, tiled=True)]
  transfers between devices with their start and end apart: 16 -> 29, of which waited for: 7 -> 13; matrix products, arithmetic and copies ran while one was open for 5% -> 4% of each run, Pallas kernels for 0% -> 9%
where the time goes in v2:
time: 306 us; the launch traced here: 302 us
  waiting for transfers between devices  92.7 us (30%)
  starting transfers between devices  64.9 us (21%)
  blocking collectives  55.2 us (18%)
  Pallas kernels  51.3 us (17%)
  local copies, waits for them, and re-layouts  15.7 us (5%)
  between operations  14.5 us (5%)
  other arithmetic  7.67 us (3%)
    ppermute x11, waiting for transfers between devices, up(): return lax.ppermute(a, axis, shift(axis, 1))  56.4 us
    all_to_all x2, blocking collectives, in_plane(): return lax.all_to_all(a, ('x', 'y', 'c'), 0, 0, tiled=True)  46.7 us
    all_to_all x5, waiting for transfers between devices, in_plane(): return lax.all_to_all(a, ('x', 'y', 'c'), 0, 0, tiled=True)  29.4 us
    ppermute x11, starting transfers between devices, down(): return lax.ppermute(a, axis, shift(axis, -1))  24.1 us
    all_to_all x5, starting transfers between devices, in_plane(): return lax.all_to_all(a, ('x', 'y', 'c'), 0, 0, tiled=True)  22 us
    pallas_call x1, Pallas kernels, pair_weights(): pl.pallas_call(pair_kernel, out_shape=(pltpu.HBM((SLAB, D), BF16), pltpu....  18.5 us
    pallas_call x5, Pallas kernels, add_credits(): pl.pallas_call(functools.partial(add_kernel, count, tuple(ks), tuple(firs...  16.2 us
    all_to_all x1, starting transfers between devices, local(): lax.all_to_all(dense_k.reshape(BR, KEYS, NBLK), ('z', 'y', 'c'), 1, 0, ti...  11.2 us
  transfers between devices with their start and end apart: 29, of which 13 were waited for; matrix products, arithmetic and copies ran while one was open for 4% of the time, Pallas kernels for 9%

profile of v2, /device:TPU:1, one launch (start us, length us, event | category | flops | bytes accessed | tf_op | source)
XLA Modules:
  0.0 302.3 jit_solution(8892638038953972989)
XLA Ops:
  17.3 14.8 %all_to_all.75 = s32[32,1,128]{2,1,0:T(1,128)S(1)} all-to-all(s32[32,1,128]{2,1,0:T(1,128)S(1)} %bitcast.82), channel_id=1, replica_groups=mesh['z'=8,'y'=4,'c'=2,'x'=4] {'x','y','c'}, dimensions={0} | all-to-all | bytes 32768 | tf_op jit(solution)/shard_map/all_to_all | solution.py:208
  32.8 4.1 %shard_map.50 = bf16[192,16,256]{2,1,0:T(8,128)(2,1)} custom-call(s32[3,64]{1,0:T(4,128)S(1)} %pad_add_fusion.asked_ref, bf16[64,16,256]{2,1,0:T(8,128)(2,1)S(1)} %bitcast.68, bf16[64,16,256]{2,1,0:T(8,128)(2,1)S(1)} %bitcast.74, bf16[64,16,256]{2,1,0:T(8,128)(2,1)S(1)} %bitcast.73), custom_call_target="tpu_custom_call" | custom-call | bytes 3145728 | tf_op jit(solution)/shard_map/pallas_call | solution.py:44
  36.9 4.3 %all-to-all-start.1 = ((bf16[32,96,256]{2,1,0:T(8,128)(2,1)}), bf16[32,96,256]{2,1,0:T(8,128)(2,1)S(1)}, u32[]{:S(2)}, u32[]{:S(2)}) async-start(bf16[32,96,256]{2,1,0:T(8,128)(2,1)} %bitcast.12), calls=%async_computation.1 | async-start | bytes 3145728 | tf_op jit(solution)/shard_map/all_to_all | solution.py:208
  44.4 11.4 %collective-permute-done.3 = bf16[1024,256]{1,0:T(8,128)(2,1)} collective-permute-done((bf16[1024,256]{1,0:T(8,128)(2,1)S(1)}, bf16[1024,256]{1,0:T(8,128)(2,1)}, u32[]{:S(2)}, u32[]{:S(2)}) %collective-permute-start.3) | collective-permute-done | bytes 524320 | tf_op jit(solution)/shard_map/ppermute | solution.py:200
  59.3 4.7 %all-to-all-done.1 = bf16[32,96,256]{2,1,0:T(8,128)(2,1)S(1)} async-done(((bf16[32,96,256]{2,1,0:T(8,128)(2,1)}), bf16[32,96,256]{2,1,0:T(8,128)(2,1)S(1)}, u32[]{:S(2)}, u32[]{:S(2)}) %all-to-all-start.1) | async-done | bytes 1572896 | tf_op jit(solution)/shard_map/all_to_all | solution.py:208
  64.0 4.9 %all-to-all-start.2 = ((bf16[32,64,256]{2,1,0:T(8,128)(2,1)}), bf16[32,64,256]{2,1,0:T(8,128)(2,1)}, u32[]{:S(2)}, u32[]{:S(2)}) async-start(bf16[32,64,256]{2,1,0:T(8,128)(2,1)} %bitcast.16), calls=%async_computation.2 | async-start | bytes 2097152 | tf_op jit(solution)/shard_map/all_to_all | solution.py:208
  71.7 11.9 %collective-permute-done.5 = bf16[1024,256]{1,0:T(8,128)(2,1)S(1)} collective-permute-done((bf16[1024,256]{1,0:T(8,128)(2,1)}, bf16[1024,256]{1,0:T(8,128)(2,1)S(1)}, u32[]{:S(2)}, u32[]{:S(2)}) %collective-permute-start.5) | collective-permute-done | bytes 524320 | tf_op jit(solution)/shard_map/ppermute | solution.py:200
  87.1 4.6 %collective-permute-done.6 = bf16[512,256]{1,0:T(8,128)(2,1)} collective-permute-done((bf16[512,256]{1,0:T(8,128)(2,1)S(1)}, bf16[512,256]{1,0:T(8,128)(2,1)}, u32[]{:S(2)}, u32[]{:S(2)}) %collective-permute-start.6) | collective-permute-done | bytes 262176 | tf_op jit(solution)/shard_map/ppermute | solution.py:200
  97.7 32.0 %all_to_all.76 = bf16[32,96,256]{2,1,0:T(8,128)(2,1)S(1)} all-to-all(bf16[32,96,256]{2,1,0:T(8,128)(2,1)S(1)} %bitcast.65), channel_id=1, replica_groups=mesh['z'=8,'y'=4,'c'=2,'x'=4] {'x','y','c'}, dimensions={0} | all-to-all | bytes 3145728 | tf_op jit(solution)/shard_map/all_to_all | solution.py:208
  129.7 18.5 %shard_map.53 = (bf16[1024,1024]{1,0:T(8,128)(2,1)}, bf16[1024,1024]{1,0:T(8,128)(2,1)}, f32[1024,128]{1,0:T(8,128)S(1)}, f32[1,1024]{1,0:T(1,128)S(1)}, bf16[19...) custom-call(s32[64]{0:T(128)S(1)} %get-tuple-element.70.group_ref, ...), custom_call_target="tpu_custom_call" | custom-call | flops 4294967296 | bytes 14680064 | tf_op jit(solution)/shard_map/pallas_call | solution.py:112
  152.9 6.0 %shard_map.59 = bf16[4,1024,256]{2,1,0:T(8,128)(2,1)} custom-call(bf16[1024,1024]{1,0:T(8,128)(2,1)} %get-tuple-element.49.rounded_ref, bf16[1024,1024]{1,0:T(8,128)(2,1)} %get-tuple-element.50.part_ref), custom_call_target="tpu_custom_call" | custom-call | flops 2147483648 | bytes 6291456 | tf_op jit(solution)/shard_map/pallas_call | solution.py:136
  158.9 16.5 %all-to-all-done.4 = bf16[32,96,256]{2,1,0:T(8,128)(2,1)S(1)} async-done(((bf16[32,96,256]{2,1,0:T(8,128)(2,1)}), bf16[32,96,256]{2,1,0:T(8,128)(2,1)S(1)}, u32[]{:S(2)}, u32[]{:S(2)}) %all-to-all-start.4) | async-done | bytes 1572896 | tf_op jit(solution)/shard_map/all_to_all | solution.py:208
  177.3 4.6 %all-to-all-start.6 = ((bf16[32,64,256]{2,1,0:T(8,128)(2,1)}), bf16[32,64,256]{2,1,0:T(8,128)(2,1)S(1)}, u32[]{:S(2)}, u32[]{:S(2)}) async-start(bf16[32,64,256]{2,1,0:T(8,128)(2,1)} %bitcast.79), calls=%async_computation.6 | async-start | bytes 2097152 | tf_op jit(solution)/shard_map/all_to_all | solution.py:208
  184.7 6.2 %collective-permute-done.8.refs_0_ = bf16[32,16,256]{2,1,0:T(8,128)(2,1)S(1)} collective-permute-done((bf16[32,16,256]{2,1,0:T(8,128)(2,1)S(1)}, bf16[32,16,256]{2,1,0:T(8,128)(2,1)S(1)}, u32[]{:S(2)}, u32[]{:S(2)}) %collective-permute-start.8) | collective-permute-done | bytes 262176 | tf_op jit(solution)/shard_map/ppermute | solution.py:200
  195.3 8.2 %all-to-all-done.6 = bf16[32,64,256]{2,1,0:T(8,128)(2,1)S(1)} async-done(((bf16[32,64,256]{2,1,0:T(8,128)(2,1)}), bf16[32,64,256]{2,1,0:T(8,128)(2,1)S(1)}, u32[]{:S(2)}, u32[]{:S(2)}) %all-to-all-start.6) | async-done | bytes 1048608 | tf_op jit(solution)/shard_map/all_to_all | solution.py:208
  203.5 4.4 %all-to-all-start.5 = ((bf16[32,96,256]{2,1,0:T(8,128)(2,1)}), bf16[32,96,256]{2,1,0:T(8,128)(2,1)S(1)}, u32[]{:S(2)}, u32[]{:S(2)}) async-start(bf16[32,96,256]{2,1,0:T(8,128)(2,1)} %bitcast.77), calls=%async_computation.5 | async-start | bytes 3145728 | tf_op jit(solution)/shard_map/all_to_all | solution.py:208
  211.4 11.5 %collective-permute-done.10.refs_0_ = bf16[64,16,256]{2,1,0:T(8,128)(2,1)S(1)} collective-permute-done((bf16[64,16,256]{2,1,0:T(8,128)(2,1)}, bf16[64,16,256]{2,1,0:T(8,128)(2,1)S(1)}, u32[]{:S(2)}, u32[]{:S(2)}) %collective-permute-start.10) | collective-permute-done | bytes 524320 | tf_op jit(solution)/shard_map/ppermute | solution.py:200
  222.9 4.6 %shard_map.56 = (bf16[64,16,256]{2,1,0:T(8,128)(2,1)}, bf16[64,16,256]{2,1,0:T(8,128)(2,1)}) custom-call(s32[2,64]{1,0:T(2,128)S(1)} %pad_add_fusion.2.asked_ref, bf16[128,16,256]{2,1,0:T(8,128)(2,1)S(1)} %bitcast.66, bf16[64,16,256]{2,1,0:T(8,128)(2,1)S(1)} %collective-permute-done.10.refs_0_, bf16[64,16,256]{2,1,0:T(8,128)(2,1)} %collective-permute-done.11.refs_1_), custom_call_target="tpu_custom_call" | custom-call | bytes 4194304 | tf_op jit(solution)/shard_map/pallas_call | solution.py:181
  233.7 11.2 %all-to-all-start.7 = ((f32[64,1,1024]{2,1,0:T(1,128)}), f32[64,1,1024]{2,1,0:T(1,128)S(1)}, u32[]{:S(2)}, u32[]{:S(2)}) async-start(f32[64,1,1024]{2,1,0:T(1,128)} %reshape.222), calls=%async_computation.8 | async-start | bytes 524288 | tf_op jit(solution)/shard_map/all_to_all | solution.py:303
  244.9 4.3 %shard_map.57 = (bf16[64,16,256]{2,1,0:T(8,128)(2,1)}, bf16[64,16,256]{2,1,0:T(8,128)(2,1)}) custom-call(s32[3,64]{1,0:T(4,128)S(1)} %pad_add_fusion.asked_ref, bf16[192,16,256]{2,1,0:T(8,128)(2,1)S(1)} %bitcast.61, bf16[64,16,256]{2,1,0:T(8,128)(2,1)S(1)} %collective-permute-done.12.refs_0_, bf16[64,16,256]{2,1,0:T(8,128)(2,1)S(1)} %collective-permute-done.13.refs_1_), custom_call_target="tpu_custom_call" | custom-call | bytes 4194304 | tf_op jit(solution)/shard_map/pallas_call | solution.py:181
  252.3 5.7 %all-to-all-done.7 = f32[64,1,1024]{2,1,0:T(1,128)S(1)} async-done(((f32[64,1,1024]{2,1,0:T(1,128)}), f32[64,1,1024]{2,1,0:T(1,128)S(1)}, u32[]{:S(2)}, u32[]{:S(2)}) %all-to-all-start.7) | async-done | bytes 262176 | tf_op jit(solution)/shard_map/all_to_all | solution.py:303
  261.9 8.5 %psum.7 = f32[1024]{0:T(1024)S(1)} all-reduce(f32[1024]{0:T(1024)S(1)} %add.150), channel_id=1, replica_groups=mesh['z'=8,'y'=4,'c'=2,'x'=4] {'x'}, use_global_device_ids=true, to_apply=%region_5.6 | all-reduce | flops 1024 | bytes 8192 | tf_op jit(solution)/shard_map/psum | solution.py:305
  278.5 4.0 %collective-permute-done.16 = bf16[512,256]{1,0:T(8,128)(2,1)S(1)} collective-permute-done((bf16[512,256]{1,0:T(8,128)(2,1)S(1)}, bf16[512,256]{1,0:T(8,128)(2,1)S(1)}, u32[]{:S(2)}, u32[]{:S(2)}) %collective-permute-start.16) | collective-permute-done | bytes 262176 | tf_op jit(solution)/shard_map/ppermute | solution.py:200
  289.1 5.0 %collective-permute-done.19 = bf16[512,256]{1,0:T(8,128)(2,1)S(1)} collective-permute-done((bf16[512,256]{1,0:T(8,128)(2,1)S(1)}, bf16[512,256]{1,0:T(8,128)(2,1)S(1)}, u32[]{:S(2)}, u32[]{:S(2)}) %collective-permute-start.19) | collective-permute-done | bytes 262176 | tf_op jit(solution)/shard_map/ppermute | solution.py:200
  (133 shorter events, 75.9 us)
Async XLA Ops:
  8.3 24.6 %collective-permute-start.1 = (bf16[1024,256]{1,0:T(8,128)(2,1)S(1)}, bf16[1024,256]{1,0:T(8,128)(2,1)S(1)}, u32[]{:S(2)}, u32[]{:S(2)}) collective-permute-start(bf16[1024,256]{1,0:T(8,128)(2,1)S(1)} %constant_dynamic-slice_fusion), channel_id=1, source_target_pairs={{0,32},{32,64},{64,96},{96,128},{128,160},{160,192},{192,224},{224... | collective-permute-start | bytes 1572872 | tf_op jit(solution)/shard_map/ppermute | solution.py:200
  10.8 22.0 %collective-permute-start = (bf16[1024,256]{1,0:T(8,128)(2,1)S(1)}, bf16[1024,256]{1,0:T(8,128)(2,1)S(1)}, u32[]{:S(2)}, u32[]{:S(2)}) collective-permute-start(bf16[1024,256]{1,0:T(8,128)(2,1)S(1)} %constant_dynamic-slice_fusion), channel_id=1, source_target_pairs={{0,224},{32,0},{64,32},{96,64},{128,96},{160,128},{192,160},{224,1... | collective-permute-start | bytes 1572872 | tf_op jit(solution)/shard_map/ppermute | solution.py:204
  36.9 27.1 %all-to-all-start.1 = ((bf16[32,96,256]{2,1,0:T(8,128)(2,1)}), bf16[32,96,256]{2,1,0:T(8,128)(2,1)S(1)}, u32[]{:S(2)}, u32[]{:S(2)}) async-start(bf16[32,96,256]{2,1,0:T(8,128)(2,1)} %bitcast.12), calls=%async_computation.1 | async-start | bytes 3145728 | tf_op jit(solution)/shard_map/all_to_all | solution.py:208
  41.2 14.6 %collective-permute-start.3 = (bf16[1024,256]{1,0:T(8,128)(2,1)S(1)}, bf16[1024,256]{1,0:T(8,128)(2,1)}, u32[]{:S(2)}, u32[]{:S(2)}) collective-permute-start(bf16[1024,256]{1,0:T(8,128)(2,1)S(1)} %collective-permute-done.1), channel_id=1, source_target_pairs={{0,32},{32,64},{64,96},{96,128},{128,160},{160,192},{192,224},{224... | collective-permute-start | bytes 1572872 | tf_op jit(solution)/shard_map/ppermute | solution.py:200
  41.3 14.5 %collective-permute-start.2 = (bf16[1024,256]{1,0:T(8,128)(2,1)S(1)}, bf16[1024,256]{1,0:T(8,128)(2,1)S(1)}, u32[]{:S(2)}, u32[]{:S(2)}) collective-permute-start(bf16[1024,256]{1,0:T(8,128)(2,1)S(1)} %collective-permute-done), channel_id=1, source_target_pairs={{0,224},{32,0},{64,32},{96,64},{128,96},{160,128},{192,160},{224,1... | collective-permute-start | bytes 1572872 | tf_op jit(solution)/shard_map/ppermute | solution.py:204
  64.0 33.7 %all-to-all-start.2 = ((bf16[32,64,256]{2,1,0:T(8,128)(2,1)}), bf16[32,64,256]{2,1,0:T(8,128)(2,1)}, u32[]{:S(2)}, u32[]{:S(2)}) async-start(bf16[32,64,256]{2,1,0:T(8,128)(2,1)} %bitcast.16), calls=%async_computation.2 | async-start | bytes 2097152 | tf_op jit(solution)/shard_map/all_to_all | solution.py:208
  68.9 14.7 %collective-permute-start.5 = (bf16[1024,256]{1,0:T(8,128)(2,1)}, bf16[1024,256]{1,0:T(8,128)(2,1)S(1)}, u32[]{:S(2)}, u32[]{:S(2)}) collective-permute-start(bf16[1024,256]{1,0:T(8,128)(2,1)} %collective-permute-done.3), channel_id=1, source_target_pairs={{0,32},{32,64},{64,96},{96,128},{128,160},{160,192},{192,224},{224... | collective-permute-start | bytes 1572872 | tf_op jit(solution)/shard_map/ppermute | solution.py:200
  69.0 14.7 %collective-permute-start.4 = (bf16[1024,256]{1,0:T(8,128)(2,1)S(1)}, bf16[1024,256]{1,0:T(8,128)(2,1)S(1)}, u32[]{:S(2)}, u32[]{:S(2)}) collective-permute-start(bf16[1024,256]{1,0:T(8,128)(2,1)S(1)} %collective-permute-done.2), channel_id=1, source_target_pairs={{0,224},{32,0},{64,32},{96,64},{128,96},{160,128},{192,160},{224,1... | collective-permute-start | bytes 1572872 | tf_op jit(solution)/shard_map/ppermute | solution.py:204
  149.1 26.3 %all-to-all-start.4 = ((bf16[32,96,256]{2,1,0:T(8,128)(2,1)}), bf16[32,96,256]{2,1,0:T(8,128)(2,1)S(1)}, u32[]{:S(2)}, u32[]{:S(2)}) async-start(bf16[32,96,256]{2,1,0:T(8,128)(2,1)} %bitcast.78), calls=%async_computation.4 | async-start | bytes 3145728 | tf_op jit(solution)/shard_map/all_to_all | solution.py:208
  152.8 121.3 %reduce-scatter.2.cloned.1.call-start = ((), (), s32[]{:S(2)}) async-start(), calls=%async_computation.9 | async-start | bytes 2621440 | tf_op jit(solution)/shard_map/reduce_scatter | solution.py:274
  177.3 26.2 %all-to-all-start.6 = ((bf16[32,64,256]{2,1,0:T(8,128)(2,1)}), bf16[32,64,256]{2,1,0:T(8,128)(2,1)S(1)}, u32[]{:S(2)}, u32[]{:S(2)}) async-start(bf16[32,64,256]{2,1,0:T(8,128)(2,1)} %bitcast.79), calls=%async_computation.6 | async-start | bytes 2097152 | tf_op jit(solution)/shard_map/all_to_all | solution.py:208
  181.9 8.9 %collective-permute-start.8 = (bf16[32,16,256]{2,1,0:T(8,128)(2,1)S(1)}, bf16[32,16,256]{2,1,0:T(8,128)(2,1)S(1)}, u32[]{:S(2)}, u32[]{:S(2)}) collective-permute-start(bf16[32,16,256]{2,1,0:T(8,128)(2,1)S(1)} %get-tuple-element.33), channel_id=1, source_target_pairs={{0,32},{32,64},{64,96},{96,128},{128,160},{160,192},{192,224},{224... | collective-permute-start | bytes 786440 | tf_op jit(solution)/shard_map/ppermute | solution.py:200
  182.0 8.8 %collective-permute-start.9 = (bf16[32,16,256]{2,1,0:T(8,128)(2,1)S(1)}, bf16[32,16,256]{2,1,0:T(8,128)(2,1)S(1)}, u32[]{:S(2)}, u32[]{:S(2)}) collective-permute-start(bf16[32,16,256]{2,1,0:T(8,128)(2,1)S(1)} %get-tuple-element.34), channel_id=1, source_target_pairs={{0,224},{32,0},{64,32},{96,64},{128,96},{160,128},{192,160},{224,1... | collective-permute-start | bytes 786440 | tf_op jit(solution)/shard_map/ppermute | solution.py:204
  203.5 30.1 %all-to-all-start.5 = ((bf16[32,96,256]{2,1,0:T(8,128)(2,1)}), bf16[32,96,256]{2,1,0:T(8,128)(2,1)S(1)}, u32[]{:S(2)}, u32[]{:S(2)}) async-start(bf16[32,96,256]{2,1,0:T(8,128)(2,1)} %bitcast.77), calls=%async_computation.5 | async-start | bytes 3145728 | tf_op jit(solution)/shard_map/all_to_all | solution.py:208
  208.0 14.9 %collective-permute-start.10 = (bf16[64,16,256]{2,1,0:T(8,128)(2,1)}, bf16[64,16,256]{2,1,0:T(8,128)(2,1)S(1)}, u32[]{:S(2)}, u32[]{:S(2)}) collective-permute-start(bf16[64,16,256]{2,1,0:T(8,128)(2,1)} %copy-done.10), channel_id=1, source_target_pairs={{0,32},{32,64},{64,96},{96,128},{128,160},{160,192},{192,224},{224... | collective-permute-start | bytes 1572872 | tf_op jit(solution)/shard_map/ppermute | solution.py:200
  208.8 14.1 %collective-permute-start.11 = (bf16[64,16,256]{2,1,0:T(8,128)(2,1)}, bf16[64,16,256]{2,1,0:T(8,128)(2,1)}, u32[]{:S(2)}, u32[]{:S(2)}) collective-permute-start(bf16[64,16,256]{2,1,0:T(8,128)(2,1)} %copy-done.9), channel_id=1, source_target_pairs={{0,224},{32,0},{64,32},{96,64},{128,96},{160,128},{192,160},{224,1... | collective-permute-start | bytes 1572872 | tf_op jit(solution)/shard_map/ppermute | solution.py:204
  227.5 17.3 %collective-permute-start.12 = (bf16[64,16,256]{2,1,0:T(8,128)(2,1)}, bf16[64,16,256]{2,1,0:T(8,128)(2,1)S(1)}, u32[]{:S(2)}, u32[]{:S(2)}) collective-permute-start(bf16[64,16,256]{2,1,0:T(8,128)(2,1)} %get-tuple-element.45), channel_id=1, source_target_pairs={{0,32},{32,64},{64,96},{96,128},{128,160},{160,192},{192,224},{224... | collective-permute-start | bytes 1572872 | tf_op jit(solution)/shard_map/ppermute | solution.py:200
  229.8 15.0 %collective-permute-start.13 = (bf16[64,16,256]{2,1,0:T(8,128)(2,1)}, bf16[64,16,256]{2,1,0:T(8,128)(2,1)S(1)}, u32[]{:S(2)}, u32[]{:S(2)}) collective-permute-start(bf16[64,16,256]{2,1,0:T(8,128)(2,1)} %get-tuple-element.46), channel_id=1, source_target_pairs={{0,224},{32,0},{64,32},{96,64},{128,96},{160,128},{192,160},{224,1... | collective-permute-start | bytes 1572872 | tf_op jit(solution)/shard_map/ppermute | solution.py:204
  233.7 24.4 %all-to-all-start.7 = ((f32[64,1,1024]{2,1,0:T(1,128)}), f32[64,1,1024]{2,1,0:T(1,128)S(1)}, u32[]{:S(2)}, u32[]{:S(2)}) async-start(f32[64,1,1024]{2,1,0:T(1,128)} %reshape.222), calls=%async_computation.8 | async-start | bytes 524288 | tf_op jit(solution)/shard_map/all_to_all | solution.py:303
  249.1 21.2 %collective-permute-start.14 = (bf16[64,16,256]{2,1,0:T(8,128)(2,1)}, bf16[64,16,256]{2,1,0:T(8,128)(2,1)S(1)}, u32[]{:S(2)}, u32[]{:S(2)}) collective-permute-start(bf16[64,16,256]{2,1,0:T(8,128)(2,1)} %get-tuple-element.47), channel_id=1, source_target_pairs={{0,32},{32,64},{64,96},{96,128},{128,160},{160,192},{192,224},{224... | collective-permute-start | bytes 1572872 | tf_op jit(solution)/shard_map/ppermute | solution.py:200
  250.6 19.8 %collective-permute-start.15 = (bf16[64,16,256]{2,1,0:T(8,128)(2,1)}, bf16[64,16,256]{2,1,0:T(8,128)(2,1)S(1)}, u32[]{:S(2)}, u32[]{:S(2)}) collective-permute-start(bf16[64,16,256]{2,1,0:T(8,128)(2,1)} %get-tuple-element.48), channel_id=1, source_target_pairs={{0,224},{32,0},{64,32},{96,64},{128,96},{160,128},{192,160},{224,1... | collective-permute-start | bytes 1572872 | tf_op jit(solution)/shard_map/ppermute | solution.py:204
  278.5 8.7 %collective-permute-start.17 = (bf16[512,256]{1,0:T(8,128)(2,1)S(1)}, bf16[512,256]{1,0:T(8,128)(2,1)S(1)}, u32[]{:S(2)}, u32[]{:S(2)}) collective-permute-start(bf16[512,256]{1,0:T(8,128)(2,1)S(1)} %get-tuple-element.59), channel_id=1, source_target_pairs={{0,3},{1,0},{2,1},{3,2},{4,7},{5,4},{6,5},{7,6},{8,11},{9,8},{10,9... | collective-permute-start | bytes 786440 | tf_op jit(solution)/shard_map/ppermute | solution.py:204
  282.8 11.3 %collective-permute-start.19 = (bf16[512,256]{1,0:T(8,128)(2,1)S(1)}, bf16[512,256]{1,0:T(8,128)(2,1)S(1)}, u32[]{:S(2)}, u32[]{:S(2)}) collective-permute-start(bf16[512,256]{1,0:T(8,128)(2,1)S(1)} %get-tuple-element.58), channel_id=1, source_target_pairs={{0,1},{1,2},{2,3},{3,0},{4,5},{5,6},{6,7},{7,4},{8,9},{9,10},{10,1... | collective-permute-start | bytes 786440 | tf_op jit(solution)/shard_map/ppermute | solution.py:200
  283.5 10.7 %collective-permute-start.21 = (bf16[512,256]{1,0:T(8,128)(2,1)S(1)}, bf16[512,256]{1,0:T(8,128)(2,1)S(1)}, u32[]{:S(2)}, u32[]{:S(2)}) collective-permute-start(bf16[512,256]{1,0:T(8,128)(2,1)S(1)} %collective-permute-done.20), channel_id=1, source_target_pairs={{0,3},{1,0},{2,1},{3,2},{4,7},{5,4},{6,5},{7,6},{8,11},{9,8},{10,9... | collective-permute-start | bytes 786440 | tf_op jit(solution)/shard_map/ppermute | solution.py:204
  (18 other events, 115.8 us)
Sparse Core Ops, SparseCore 0:
  159.1 41.2 reduce-scatter.1
